TPU v7x, 32 devices: a whole 2x2x4 slice. The times are simulated.
32 devices in a mesh: req: 8 (over z, y), head: 4 (over x, core).
Axes of the slice: x: 2, y: 2, z: 4, core: 2. Of those that a mesh axis runs over, the one named last changes fastest.
Arguments:
- tokens: bfloat16 [8192, 1024], P(('req', 'head')), may hold values from -6 to 6
- w_proj: bfloat16 [1024, 2048], P(None, 'head'), may hold values from -0.1875 to 0.1875
- w_out: bfloat16 [1024, 1024], replicated, may hold values from -0.1875 to 0.1875
- kv_cache: bfloat16 [8, 8, 12, 128, 2048], P('req', None, None, None, 'head'), may hold values from -6 to 6
- slot_request: int32 [16], P('req'), may hold values from 0 to 15, each once
- lengths: int32 [16], replicated, may hold values from 1 to 4096
- block_owner: int32 [512, 1], P('req'), may hold values from 0 to 7; in each aligned block of 64 rows (0 to 63, 64 to 127, ...) at most 12 rows name the same one
Outputs:
- mixed: bfloat16 [8192, 1024], P(('req', 'head'))
Inputs may be any that keep to these rules, and one draw needn't show every extreme that they name: `block_owner`: within each aligned block of 64 rows no owner appears more than 12 times.
All inputs are finite; a program needn't handle non-finite values.
Results may differ from a plain program's by a relative error of at most 0.0088.
Values may be sent and summed in bfloat16 or wider, within the bound.
A program may use at most 128 MiB of HBM per device.

v0:
```python
import jax
import jax.numpy as jnp
from jax import lax
from jax.sharding import PartitionSpec as P

DH = 64
CAND = 512
BLK = 128
MAXB = 32


def layer_norm(values):
    mean = jnp.mean(values, axis=-1, keepdims=True)
    square = jnp.mean(values * values, axis=-1, keepdims=True)
    return (values - mean) * lax.rsqrt(square - mean * mean + 1e-05)


def shards(tokens, w_proj, w_out, kv_cache, slot_request, lengths, block_owner):
    head_local = w_proj.shape[1] // (2 * DH)
    gathered = lax.all_gather(tokens, "head", axis=0, tiled=True)
    normed = layer_norm(gathered.astype(jnp.float32)).astype(jnp.bfloat16)
    row_count = normed.shape[0]
    slots = row_count // CAND
    proj = jax.nn.silu(jnp.dot(normed, w_proj, preferred_element_type=jnp.float32))
    proj = proj.reshape(row_count, head_local, 2, DH)
    gate_u = proj[:, :, 0].astype(jnp.bfloat16).reshape(row_count, head_local * DH)
    query = proj[:, :, 1].astype(jnp.bfloat16).reshape(slots, CAND, head_local, DH)
    received = lax.all_to_all(kv_cache, "req", split_axis=1, concat_axis=0, tiled=True)
    most_slots = received.shape[2]
    pool = received.reshape(-1, BLK, received.shape[-1])
    owner_count = lax.axis_size("req")
    owners = block_owner[:, 0]
    onehot = (owners[:, None] == jnp.arange(owner_count, dtype=jnp.int32)[None, :]).astype(
        jnp.int32
    )
    rank = jnp.sum((jnp.cumsum(onehot, axis=0) - onehot) * onehot, axis=1)
    history = pool[owners * most_slots + rank].reshape(slots, MAXB * BLK, head_local, 2, DH)
    total_requests = lengths.shape[0]
    match = slot_request[:, None] == jnp.arange(total_requests, dtype=jnp.int32)[None, :]
    slot_lengths = jnp.sum(jnp.where(match, lengths[None, :], 0), axis=1)
    positions = jnp.arange(MAXB * BLK, dtype=jnp.int32)
    scale = 1.0 / DH**0.5
    results = []
    for slot in range(slots):
        keys = history[slot, :, :, 0]
        values = history[slot, :, :, 1]
        scores = (
            jnp.einsum("chd,phd->hcp", query[slot], keys, preferred_element_type=jnp.float32)
            * scale
        )
        live = positions < slot_lengths[slot]
        weights = jnp.where(live[None, None, :], jax.nn.silu(scores), 0.0).astype(jnp.bfloat16)
        results.append(
            jnp.einsum("hcp,phd->chd", weights, values, preferred_element_type=jnp.float32)
        )
    attn = jnp.stack(results).reshape(row_count, head_local * DH).astype(jnp.bfloat16)
    width_all = w_out.shape[0]
    attn_wide = attn.astype(jnp.float32)
    first_sum, second_sum = lax.psum(
        (jnp.sum(attn_wide, axis=1), jnp.sum(attn_wide * attn_wide, axis=1)), "head"
    )
    mean = (first_sum / width_all)[:, None]
    square = (second_sum / width_all)[:, None]
    hidden = (
        (attn_wide - mean) * lax.rsqrt(square - mean * mean + 1e-05) * gate_u.astype(jnp.float32)
    )
    hidden = hidden.astype(jnp.bfloat16)
    local_width = head_local * DH
    w_rows = lax.dynamic_slice_in_dim(w_out, lax.axis_index("head") * local_width, local_width, 0)
    summed = lax.psum_scatter(
        jnp.dot(hidden, w_rows, preferred_element_type=jnp.float32),
        "head",
        scatter_dimension=0,
        tiled=True,
    )
    return summed.astype(jnp.bfloat16)


def solution(mesh):
    return jax.shard_map(
        shards,
        mesh=mesh,
        in_specs=(
            P(("req", "head"), None),
            P(None, "head"),
            P(),
            P("req", None, None, None, "head"),
            P("req"),
            P(),
            P("req", None),
        ),
        out_specs=P(("req", "head"), None),
        check_vma=False,
    )
```

profile of v0, /device:TPU:0, one launch (start us, length us, event | category | flops | bytes accessed | tf_op | source)
XLA Modules:
  0.0 528.5 jit_solution(8174907164067248157)
XLA Ops:
  6.5 7.4 %all-to-all-start = ((bf16[1,8,12,128,512]{4,3,2,0,1:T(8,128)(2,1)}), bf16[1,8,12,128,512]{4,3,2,0,1:T(8,128)(2,1)}, u32[]{:S(2)}, u32[]{:S(2)}) async-start(bf16[1,8,12,128,512]{4,3,2,0,1:T(8,128)(2,1)} %bitcast.66), calls=%async_computation | async-start | bytes 25165824 | tf_op jit(solution)/shard_map/all_to_all | solution.py:28
  14.0 0.7 all-gather.2.cloned.1.call-update
  14.7 0.0 reduce-scatter.2.cloned.1.call-start
  14.8 0.1 fusion.38
  14.8 0.1 reduce_window_sum.11
  14.9 0.2 select_reduce_fusion
  15.2 0.2 fusion.39
  15.3 0.7 fusion.50
  16.0 0.7 iota_compare_fusion.2
  16.6 0.6 iota_compare_fusion.1
  17.3 23.1 %all-gather.2.cloned.1.call-done = bf16[1024,1024]{1,0:T(8,128)(2,1)} async-done(((bf16[256,1024]{1,0:T(8,128)(2,1)}), bf16[1024,1024]{1,0:T(8,128)(2,1)}) %all-gather.2.cloned.1.call-update) | async-done | bytes 2097168 | tf_op jit(solution)/shard_map/all_gather | solution.py:20
  40.4 2.3 convert_reduce_fusion
  42.7 3.7 multiply_convert_fusion
  46.4 0.9 slice.59
  47.3 239.7 %all-to-all-done = bf16[1,8,12,128,512]{4,3,2,0,1:T(8,128)(2,1)} async-done(((bf16[1,8,12,128,512]{4,3,2,0,1:T(8,128)(2,1)}), bf16[1,8,12,128,512]{4,3,2,0,1:T(8,128)(2,1)}, u32[]{:S(2)}, u32[]{:S(2)}) %all-to-all-start) | async-done | bytes 12582944 | tf_op jit(solution)/shard_map/all_to_all | solution.py:28
  287.0 10.3 %gather_fusion = bf16[64,128,512]{2,1,0:T(8,128)(2,1)} fusion(bf16[96,128,512]{2,1,0:T(8,128)(2,1)} %bitcast.1, s32[1024]{0:T(1024)S(1)} %pad_clamp_fusion), kind=kCustom, calls=%fused_computation | custom fusion | bytes 16777472 | tf_op jit(solution)/shard_map/gather | solution.py:37
  297.3 30.3 %reshape.81 = bf16[2,4096,4,2,64]{4,3,2,1,0:T(2,128)(2,1)} reshape(bf16[64,128,512]{2,1,0:T(8,128)(2,1)} %gather_fusion) | data formatting | bytes 16777216 | tf_op jit(solution)/shard_map/reshape | solution.py:37
  327.6 32.9 %fusion.49 = (bf16[1,4096,4,1,64]{4,3,2,1,0:T(2,128)(2,1)}, bf16[1,4096,4,1,64]{4,3,2,1,0:T(2,128)(2,1)}, bf16[1,4096,4,1,64]{4,3,2,1,0:T(2,128)(2,1)}, bf16[1,4096,4,1,64]{4,3,2,1,0:T(2,128)(2,1)}) fusion(bf16[2,4096,4,2,64]{4,3,2,1,0:T(2,128)(2,1)} %reshape.81), kind=kLoop, calls=%fused_computation.57 | loop fusion | bytes 16777216 | tf_op jit(solution)/shard_map/slice | solution.py:46
  360.5 17.8 %copy.45 = bf16[1,4096,4,1,64]{1,4,2,3,0:T(8,128)(2,1)} copy(bf16[1,4096,4,1,64]{4,3,2,1,0:T(2,128)(2,1)} %get-tuple-element.11) | data formatting | bytes 4194304
  378.4 17.8 %copy.47 = bf16[1,4096,4,1,64]{1,4,2,3,0:T(8,128)(2,1)} copy(bf16[1,4096,4,1,64]{4,3,2,1,0:T(2,128)(2,1)} %get-tuple-element.13) | data formatting | bytes 4194304
  396.1 17.8 %copy.48 = bf16[1,4096,4,1,64]{1,4,2,3,0:T(8,128)(2,1)} copy(bf16[1,4096,4,1,64]{4,3,2,1,0:T(2,128)(2,1)} %get-tuple-element.12) | data formatting | bytes 4194304
  413.9 17.8 %copy.50 = bf16[1,4096,4,1,64]{1,4,2,3,0:T(8,128)(2,1)} copy(bf16[1,4096,4,1,64]{4,3,2,1,0:T(2,128)(2,1)} %get-tuple-element.14) | data formatting | bytes 4194304
  431.7 16.4 %fusion.24 = bf16[1,512,4,64]{1,3,2,0:T(8,128)(2,1)S(1)} fusion(pred[4096]{0:T(1024)(128)(4,1)S(1)} %iota_compare_fusion.2, bf16[1,4096,4,1,64]{1,4,2,3,0:T(8,128)(2,1)} %copy.47, bf16[1,4096,4,1,64]{1,4,2,3,0:T(8,128)(2,1)} %copy.45, bf16[1024,4,2,64]{0,3,2,1:T(8,128)(2,1)S(1)} %bitcast.71), kind=kOutput, calls=%fused_computation.22 | convolution fusion | flops 2206203904 | bytes 4722688 | tf_op jit(solution)/shard_map/hcp,phd->chd/dot_general | solution.py:54
  448.1 16.6 %fusion.19 = bf16[1,512,4,64]{1,3,2,0:T(8,128)(2,1)S(1)} fusion(pred[4096]{0:T(1024)(128)(4,1)S(1)} %iota_compare_fusion.1, bf16[1,4096,4,1,64]{1,4,2,3,0:T(8,128)(2,1)} %copy.50, bf16[1,4096,4,1,64]{1,4,2,3,0:T(8,128)(2,1)} %copy.48, bf16[1024,4,2,64]{0,3,2,1:T(8,128)(2,1)} %bitcast.72), kind=kOutput, calls=%fused_computation.21 | convolution fusion | flops 2206203904 | bytes 4722688 | tf_op jit(solution)/shard_map/hcp,phd->chd/dot_general | solution.py:54
  464.7 0.2 fusion.48
  464.8 0.1 fusion.34
  464.9 0.8 copy.42
  465.8 0.2 copy.51
  466.0 5.8 %all-reduce = (f32[1024]{0:T(1024)S(1)}, f32[1024]{0:T(1024)S(1)}) all-reduce(f32[1024]{0:T(1024)S(1)} %bitcast.76, f32[1024]{0:T(1024)S(1)} %bitcast.75), channel_id=1, replica_groups=mesh['req'=8,'head'=4] {'head'}, use_global_device_ids=true, to_apply=%region_8.9 | all-reduce | flops 2048 | bytes 16384 | tf_op jit(solution)/shard_map/psum | solution.py:59
  471.8 3.8 fusion.32
  475.5 44.0 %reduce-scatter.2.cloned.1.call-done = f32[256,1024]{1,0:T(8,128)} async-done(((f32[1024,1024]{1,0:T(8,128)}), f32[256,1024]{1,0:T(8,128)}) %reduce-scatter.2.cloned.1.call-update) | async-done | bytes 1048592 | tf_op jit(solution)/shard_map/reduce_scatter | solution.py:70
  519.5 2.1 convert_element_type.60
  (18 shorter events, 0.1 us)
Async XLA Ops:
  6.5 465.2 %copy-start = (bf16[1024,1024]{1,0:T(8,128)(2,1)S(1)}, bf16[1024,1024]{1,0:T(8,128)(2,1)}, u32[]{:S(2)}) copy-start(bf16[1024,1024]{1,0:T(8,128)(2,1)} %param.9) | copy-start | bytes 6291460
  6.5 8.2 %copy-start.2 = (s32[64,1]{0,1:T(1,128)S(1)}, s32[64,1]{0,1:T(1,128)}, u32[]{:S(2)}) copy-start(s32[64,1]{0,1:T(1,128)} %param.13) | copy-start | bytes 772
  6.5 8.6 %copy-start.3 = (s32[16]{0:T(128)S(1)}, s32[16]{0:T(128)}, u32[]{:S(2)}) copy-start(s32[16]{0:T(128)} %param.12) | copy-start | bytes 196
  6.5 8.6 %copy-start.4 = (s32[2]{0:T(128)S(1)}, s32[2]{0:T(128)}, u32[]{:S(2)}) copy-start(s32[2]{0:T(128)} %param.11) | copy-start | bytes 28
  6.5 280.5 %all-to-all-start = ((bf16[1,8,12,128,512]{4,3,2,0,1:T(8,128)(2,1)}), bf16[1,8,12,128,512]{4,3,2,0,1:T(8,128)(2,1)}, u32[]{:S(2)}, u32[]{:S(2)}) async-start(bf16[1,8,12,128,512]{4,3,2,0,1:T(8,128)(2,1)} %bitcast.66), calls=%async_computation | async-start | bytes 25165824 | tf_op jit(solution)/shard_map/all_to_all | solution.py:28
  14.0 26.4 %all-gather.2.cloned.1.call-start = ((), (), s32[]{:S(2)}) async-start(), calls=%async_computation.2 | async-start | bytes 2621440 | tf_op jit(solution)/shard_map/all_gather | solution.py:20
  14.7 504.8 %reduce-scatter.2.cloned.1.call-start = ((), (), s32[]{:S(2)}) async-start(), calls=%async_computation.3 | async-start | bytes 5242880 | tf_op jit(solution)/shard_map/reduce_scatter | solution.py:70
  46.4 385.3 %copy-start.1 = (bf16[1024,512]{0,1:T(8,128)(2,1)}, bf16[1024,512]{0,1:T(8,128)(2,1)S(1)}, u32[]{:S(2)}) copy-start(bf16[1024,512]{0,1:T(8,128)(2,1)S(1)} %multiply_convert_fusion) | copy-start | bytes 3145732
Sparse Core Ops, SparseCore 0:
  16.4 23.9 all-gather.1
  475.7 43.8 reduce-scatter.1
where the time goes:
time: 531 us; the launch traced here: 528 us
  waiting for transfers between devices  308 us (58%)
  local copies, waits for them, and re-layouts  147 us (28%)
  matrix products  40.5 us (8%)
  between operations  13.6 us (3%)
  starting transfers between devices  7.49 us (1%)
  other arithmetic  6.43 us (1%)
  blocking collectives  5.77 us (1%)
    all_to_all x1, waiting for transfers between devices, shards(): lax.all_to_all(kv_cache, 'req', split_axis=1, concat_axis=0, tiled=True)  240 us
    unnamed x17, local copies, waits for them, and re-layouts  71.3 us
    reduce_scatter x1, waiting for transfers between devices, shards(): lax.psum_scatter(jnp.dot(hidden, w_rows, preferred_element_type=jnp.float...  44 us
    dot_general x2, matrix products, shards(): jnp.einsum('hcp,phd->chd', weights, values, preferred_element_type=jnp.fl...  33 us
    slice x1, local copies, waits for them, and re-layouts, shards(): values = history[slot, :, :, 1]  32.9 us
    reshape x1, local copies, waits for them, and re-layouts, shards(): pool[owners * most_slots + rank]  30.3 us
    all_gather x1, waiting for transfers between devices, shards(): gathered = lax.all_gather(tokens, 'head', axis=0, tiled=True)  23.1 us
  transfers between devices with their start and end apart: 3, of which 3 were waited for; matrix products, arithmetic and copies ran while one was open for 2% of the time, Pallas kernels for 0%

commit v1 on v0

v1 whole, which is shorter than its diff:
```python
import functools

import jax
import jax.numpy as jnp
from jax import lax
from jax.experimental import pallas as pl
from jax.experimental.pallas import tpu as pltpu
from jax.sharding import PartitionSpec as P

DH = 64
CAND = 512
BLK = 128
MAXB = 32
LANES = 2 * DH


def proj_kernel(x_ref, w_ref, gate_ref, query_ref):
    x = x_ref[...].astype(jnp.float32)
    mean = jnp.mean(x, axis=-1, keepdims=True)
    square = jnp.mean(x * x, axis=-1, keepdims=True)
    normed = ((x - mean) * lax.rsqrt(square - mean * mean + 1e-05)).astype(jnp.bfloat16)
    half = 0.5 * jnp.dot(normed, w_ref[...], preferred_element_type=jnp.float32)
    out = half + half * jnp.tanh(half)
    first = lax.broadcasted_iota(jnp.int32, (x.shape[0], LANES), 1) < DH
    for pair in range(w_ref.shape[1] // (2 * LANES)):
        even = out[:, 2 * pair * LANES : (2 * pair + 1) * LANES]
        odd = out[:, (2 * pair + 1) * LANES : (2 * pair + 2) * LANES]
        at = pl.ds(pair * LANES, LANES)
        gate_ref[:, at] = jnp.where(first, even, pltpu.roll(odd, DH, 1)).astype(jnp.bfloat16)
        query = jnp.where(first, pltpu.roll(even, DH, 1), odd).astype(jnp.bfloat16)
        query_ref[:, at] = query * jnp.bfloat16(0.5 / DH**0.5)


def project(tokens, w_proj):
    rows, width = tokens.shape
    columns = w_proj.shape[1] // 2
    step = 256
    out = jax.ShapeDtypeStruct((rows, columns), jnp.bfloat16)
    return pl.pallas_call(
        proj_kernel,
        grid=(rows // step,),
        out_shape=(out, out),
        in_specs=[
            pl.BlockSpec((step, width), lambda i: (i, 0)),
            pl.BlockSpec(w_proj.shape, lambda i: (0, 0)),
        ],
        out_specs=[pl.BlockSpec((step, columns), lambda i: (i, 0))] * 2,
        compiler_params=pltpu.CompilerParams(vmem_limit_bytes=32 * 2**20),
        cost_estimate=pl.CostEstimate(
            flops=4 * rows * width * columns, bytes_accessed=4 * rows * width, transcendentals=0
        ),
    )(tokens, w_proj)


def attend_kernel(count_ref, slot_ref, live_ref, q_ref, kv_ref, out_ref, qp_ref, acc_ref):
    d = pl.program_id(0)
    n = count_ref[d]
    heads = q_ref.shape[2] // DH
    first = lax.broadcasted_iota(jnp.int32, (q_ref.shape[1], LANES), 1) < DH
    for pair in range(heads // 2):
        packed = q_ref[0, :, pair * LANES : (pair + 1) * LANES].astype(jnp.float32)
        even = jnp.where(first, packed, 0.0)
        odd = jnp.where(first, pltpu.roll(packed, DH, 1), 0.0)
        qp_ref[2 * pair] = even.astype(jnp.bfloat16)
        qp_ref[2 * pair + 1] = odd.astype(jnp.bfloat16)
    acc_ref[...] = jnp.zeros_like(acc_ref)
    event = lax.broadcasted_iota(jnp.int32, (BLK, LANES), 0)

    @pl.loop(0, (n + 1) // 2)
    def _(step):
        k0, k1 = slot_ref[d, 2 * step], slot_ref[d, 2 * step + 1]
        keep0 = (event < live_ref[d, 2 * step]).astype(jnp.float32).astype(jnp.bfloat16)
        keep1 = (event < live_ref[d, 2 * step + 1]).astype(jnp.float32).astype(jnp.bfloat16)
        for h in range(heads):
            at = slice(h * LANES, (h + 1) * LANES)
            kv = jnp.concatenate(
                [kv_ref[0, 0, k0, :, at] * keep0, kv_ref[0, 0, k1, :, at] * keep1], axis=0
            )
            half = lax.dot_general(
                qp_ref[h], kv, (((1,), (1,)), ((), ())), preferred_element_type=jnp.float32
            )
            weights = (half + half * jnp.tanh(half)).astype(jnp.bfloat16)
            acc_ref[h] += jnp.dot(weights, kv, preferred_element_type=jnp.float32)

    for pair in range(heads // 2):
        even, odd = acc_ref[2 * pair], acc_ref[2 * pair + 1]
        out_ref[0, :, pair * LANES : (pair + 1) * LANES] = jnp.where(
            first, pltpu.roll(even, DH, 1), odd
        ).astype(jnp.bfloat16)


def attend(count, slot, live, queries, kv_cache):
    scorers, rows, width = queries.shape
    heads = width // DH
    most = kv_cache.shape[2]
    flops = scorers * rows * most * BLK * width
    return pl.pallas_call(
        attend_kernel,
        grid_spec=pltpu.PrefetchScalarGridSpec(
            num_scalar_prefetch=3,
            grid=(scorers,),
            in_specs=[
                pl.BlockSpec((1, rows, width), lambda d, *_: (d, 0, 0)),
                pl.BlockSpec((1, 1) + kv_cache.shape[2:], lambda d, *_: (0, d, 0, 0, 0)),
            ],
            out_specs=pl.BlockSpec((1, rows, width), lambda d, *_: (d, 0, 0)),
            scratch_shapes=[
                pltpu.VMEM((heads, rows, LANES), jnp.bfloat16),
                pltpu.VMEM((heads, rows, LANES), jnp.float32),
            ],
        ),
        out_shape=jax.ShapeDtypeStruct(queries.shape, jnp.bfloat16),
        compiler_params=pltpu.CompilerParams(vmem_limit_bytes=40 * 2**20),
        cost_estimate=pl.CostEstimate(
            flops=8 * flops, bytes_accessed=kv_cache.size * 2, transcendentals=0
        ),
    )(count, slot, live, queries, kv_cache)


def tables(slot_request, lengths, block_owner, most, slots):
    total = lengths.shape[0]
    match = slot_request[:, None] == jnp.arange(total, dtype=jnp.int32)[None, :]
    slot_lengths = jnp.sum(jnp.where(match, lengths[None, :], 0), axis=1)
    starts = jnp.arange(MAXB, dtype=jnp.int32) * BLK
    live = jnp.clip(slot_lengths[:, None] - starts[None, :], 0, BLK).reshape(-1)
    both = lax.all_gather(jnp.stack([block_owner[:, 0], live]), "req", axis=0)
    owners, live = both[:, 0], both[:, 1]
    mine = owners == lax.axis_index("req")
    row = jnp.arange(owners.shape[1], dtype=jnp.int32)
    earlier = row[None, :] < row[:, None]
    rank = jnp.sum((mine[:, None, :] & earlier[None]).astype(jnp.int32), axis=2)
    used = mine & (live > 0)
    made = []
    wide = most + most % 2
    for slot in range(slots):
        here = used & (row // MAXB == slot)[None]
        place = jnp.sum((here[:, None, :] & earlier[None]).astype(jnp.int32), axis=2)
        hit = here[:, None, :] & (
            place[:, None, :] == jnp.arange(wide, dtype=jnp.int32)[None, :, None]
        )
        made.append(
            (
                jnp.sum(here.astype(jnp.int32), axis=1),
                jnp.sum(jnp.where(hit, rank[:, None, :], 0), axis=2),
                jnp.sum(jnp.where(hit, live[:, None, :], 0), axis=2),
            )
        )
    return made


def finish(attn, gate, w_out):
    wide = attn.astype(jnp.float32)
    mean = jnp.mean(wide, axis=-1, keepdims=True)
    square = jnp.mean(wide * wide, axis=-1, keepdims=True)
    hidden = (wide - mean) * lax.rsqrt(square - mean * mean + 1e-05) * gate.astype(jnp.float32)
    return jnp.dot(
        hidden.astype(jnp.bfloat16), w_out, preferred_element_type=jnp.float32
    ).astype(jnp.bfloat16)


def shards(tokens, w_proj, w_out, kv_cache, slot_request, lengths, block_owner):
    gathered = lax.all_gather(tokens, "head", axis=0, tiled=True)
    slots = gathered.shape[0] // CAND
    made = tables(slot_request, lengths, block_owner, kv_cache.shape[2], slots)
    gate, query = project(gathered, w_proj)
    sums = []
    for slot in range(slots):
        queries = lax.all_gather(query[slot * CAND : (slot + 1) * CAND], "req", axis=0)
        part = attend(*made[slot], queries, kv_cache)
        sums.append(lax.psum_scatter(part, "req", scatter_dimension=0, tiled=False))
    attn = jnp.concatenate(sums, axis=0)
    attn = lax.all_to_all(attn, "head", split_axis=0, concat_axis=1, tiled=True)
    gate = lax.all_to_all(gate, "head", split_axis=0, concat_axis=1, tiled=True)
    return finish(attn, gate, w_out)


def solution(mesh):
    return jax.shard_map(
        shards,
        mesh=mesh,
        in_specs=(
            P(("req", "head"), None),
            P(None, "head"),
            P(),
            P("req", None, None, None, "head"),
            P("req"),
            P(),
            P("req", None),
        ),
        out_specs=P(("req", "head"), None),
        check_vma=False,
    )
```

time: 531 us -> 316 us (0.60)
  local copies, waits for them, and re-layouts: 147 us -> 11.9 us
  waiting for transfers between devices: 308 us -> 232 us
  matrix products: 40.5 us -> 1.52 us
  Pallas kernels: 0 us -> 25.8 us
  blocking collectives: 5.77 us -> 20.5 us
    all_to_all x1 -> x2, waiting for transfers between devices: 240 us -> 16.4 us  [the longest x1 8.62 us: shards(): gate = lax.all_to_all(gate, 'head', split_axis=0, concat_axis=1, tiled=True)]
    reduce_scatter x1 -> x2, waiting for transfers between devices: 44 us -> 126 us  [shards(): sums.append(lax.psum_scatter(part, 'req', scatter_dimension=0, tiled=False))]
    unnamed x17 -> x20, local copies, waits for them, and re-layouts: 71.3 us -> 8.64 us
    all_gather x0 -> x2, waiting for transfers between devices: none -> 61.4 us  [shards(): lax.all_gather(query[slot * CAND:(slot + 1) * CAND], 'req', axis=0)]
    dot_general x4 -> x1, matrix products: 40.5 us -> 1.52 us  [finish(): jnp.dot(hidden.astype(jnp.bfloat16), w_out, preferred_element_type=jnp.fl...]
    slice x3 -> x2, local copies, waits for them, and re-layouts: 34.5 us -> 0.83 us  [the longest x1 0.82 us: shards(): query[slot * CAND:(slot + 1) * CAND]]
    reshape x1 -> x0, local copies, waits for them, and re-layouts: 30.3 us -> none  [shards(): pool[owners * most_slots + rank]]
    pallas_call x0 -> x3, Pallas kernels: none -> 25.8 us  [the longest x2 23 us: attend(): pl.pallas_call(attend_kernel, grid_spec=pltpu.PrefetchScalarGridSpec(num_...]
  transfers between devices with their start and end apart: 3 -> 7, of which waited for: 3 -> 7; matrix products, arithmetic and copies ran while one was open for 2% -> 1% of each run, Pallas kernels for 0% -> 7%
where the time goes in v1:
time: 316 us; the launch traced here: 315 us
  waiting for transfers between devices  232 us (73%)
  Pallas kernels  25.8 us (8%)
  blocking collectives  20.5 us (6%)
  between operations  13.3 us (4%)
  local copies, waits for them, and re-layouts  11.9 us (4%)
  starting transfers between devices  7.1 us (2%)
  other arithmetic  3.29 us (1%)
    reduce_scatter x2, waiting for transfers between devices, shards(): sums.append(lax.psum_scatter(part, 'req', scatter_dimension=0, tiled=False))  126 us
    all_gather x2, waiting for transfers between devices, shards(): lax.all_gather(query[slot * CAND:(slot + 1) * CAND], 'req', axis=0)  61.4 us
    all_gather x1, waiting for transfers between devices, shards(): gathered = lax.all_gather(tokens, 'head', axis=0, tiled=True)  26.9 us
    pallas_call x2, Pallas kernels, attend(): pl.pallas_call(attend_kernel, grid_spec=pltpu.PrefetchScalarGridSpec(num_...  23 us
    all_gather x1, blocking collectives, tables(): both = lax.all_gather(jnp.stack([block_owner[:, 0], live]), 'req', axis=0)  20.5 us
    unnamed x20, local copies, waits for them, and re-layouts  8.64 us
    all_to_all x1, waiting for transfers between devices, shards(): gate = lax.all_to_all(gate, 'head', split_axis=0, concat_axis=1, tiled=True)  8.62 us
    all_to_all x1, waiting for transfers between devices, shards(): attn = lax.all_to_all(attn, 'head', split_axis=0, concat_axis=1, tiled=True)  7.81 us
  transfers between devices with their start and end apart: 7, of which 7 were waited for; matrix products, arithmetic and copies ran while one was open for 1% of the time, Pallas kernels for 7%

profile of v1, /device:TPU:0, one launch (start us, length us, event | category | flops | bytes accessed | tf_op | source)
XLA Modules:
  0.0 315.2 jit_solution(11034486195687372580)
XLA Ops:
  6.6 0.7 all-gather.8.cloned.1.call-update
  7.3 26.9 %all-gather.8.cloned.1.call-done.x_ref = bf16[1024,1024]{1,0:T(8,128)(2,1)} async-done(((bf16[256,1024]{1,0:T(8,128)(2,1)}), bf16[1024,1024]{1,0:T(8,128)(2,1)}) %all-gather.8.cloned.1.call-update) | async-done | bytes 2097168 | tf_op jit(solution)/shard_map/all_gather | solution.py:162
  34.2 1.6 copy-done.5
  35.8 1.2 copy-done.6
  37.1 2.8 shard_map.73
  39.9 0.8 fusion.5
  40.8 0.7 all-gather.12.cloned.1.call-update
  41.5 0.2 fusion.4
  41.9 20.5 %all-gather.3 = s32[8,2,64]{2,1,0:T(2,128)S(1)} all-gather(s32[1,2,64]{2,1,0:T(2,128)S(1)} %add_bitcast_fusion), channel_id=2, replica_groups=mesh['req'=8,'head'=4] {'req'}, dimensions={0}, use_global_device_ids=true | all-gather | bytes 4608 | tf_op jit(solution)/shard_map/all_gather | solution.py:126
  62.5 0.5 convert_reduce_fusion.3
  63.0 0.9 select_reduce_fusion
  64.0 0.2 convert_reduce_fusion.5
  64.2 26.0 %all-gather.10.cloned.1.call-done = bf16[4096,256]{1,0:T(8,128)(2,1)} async-done(((bf16[512,256]{1,0:T(8,128)(2,1)}), bf16[4096,256]{1,0:T(8,128)(2,1)}) %all-gather.10.cloned.1.call-update) | async-done | bytes 2097168 | tf_op jit(solution)/shard_map/all_gather | solution.py:168
  90.2 1.6 copy-done.4
  91.8 11.5 %shard_map.74 = bf16[8,512,256]{2,1,0:T(8,128)(2,1)S(1)} custom-call(s32[8]{0:T(128)S(1)} %get-tuple-element.20.count_ref, s32[8,12]{1,0:T(8,128)S(1)} %copy.16.slot_ref, s32[8,12]{1,0:T(8,128)S(1)} %copy.17.live_ref, bf16[8,512,256]{2,1,0:T(8,128)(2,1)S(1)} %bitcast.37, bf16[1,8,12,128,512]{4,3,2,1,0:T(8,128)(2,1)} %kv_ref.3), custom_call_target="tpu_custom_call" | custom-call | flops 12884901888 | bytes 12582912 | tf_op jit(solution)/shard_map/pallas_call | solution.py:97
  103.4 1.3 copy-done.1
  105.0 35.4 %all-gather.12.cloned.1.call-done = bf16[4096,256]{1,0:T(8,128)(2,1)} async-done(((bf16[512,256]{1,0:T(8,128)(2,1)}), bf16[4096,256]{1,0:T(8,128)(2,1)}) %all-gather.12.cloned.1.call-update) | async-done | bytes 2097168 | tf_op jit(solution)/shard_map/all_gather | solution.py:168
  140.3 1.6 copy-done.3
  141.9 11.5 %shard_map.75 = bf16[8,512,256]{2,1,0:T(8,128)(2,1)S(1)} custom-call(s32[8]{0:T(128)S(1)} %get-tuple-element.21.count_ref, s32[8,12]{1,0:T(8,128)S(1)} %copy.18.slot_ref, s32[8,12]{1,0:T(8,128)S(1)} %copy.19.live_ref, bf16[8,512,256]{2,1,0:T(8,128)(2,1)S(1)} %bitcast.36, bf16[1,8,12,128,512]{4,3,2,1,0:T(8,128)(2,1)} %kv_ref.3), custom_call_target="tpu_custom_call" | custom-call | flops 12884901888 | bytes 12582912 | tf_op jit(solution)/shard_map/pallas_call | solution.py:97
  153.4 1.3 copy-done.2
  154.7 55.6 %reduce-scatter.3.cloned.1.call-done = bf16[1,512,256]{2,1,0:T(8,128)(2,1)} async-done(((bf16[8,512,256]{2,1,0:T(8,128)(2,1)}), bf16[1,512,256]{2,1,0:T(8,128)(2,1)}) %reduce-scatter.3.cloned.1.call-update) | async-done | bytes 262160 | tf_op jit(solution)/shard_map/reduce_scatter | solution.py:170
  210.3 70.0 %reduce-scatter.5.cloned.1.call-done = bf16[1,512,256]{2,1,0:T(8,128)(2,1)} async-done(((bf16[8,512,256]{2,1,0:T(8,128)(2,1)}), bf16[1,512,256]{2,1,0:T(8,128)(2,1)}) %reduce-scatter.5.cloned.1.call-update) | async-done | bytes 262160 | tf_op jit(solution)/shard_map/reduce_scatter | solution.py:170
  280.3 1.1 pad_maximum_fusion
  281.4 1.0 copy.20
  282.4 3.5 %all-to-all-start = ((bf16[4,256,256]{1,2,0:T(8,128)(2,1)}), bf16[4,256,256]{1,2,0:T(8,128)(2,1)S(1)}, u32[]{:S(2)}, u32[]{:S(2)}) async-start(bf16[4,256,256]{1,2,0:T(8,128)(2,1)} %copy.20), calls=%async_computation.2 | async-start | bytes 1048576 | tf_op jit(solution)/shard_map/all_to_all | solution.py:172
  285.9 1.0 copy.21
  286.9 7.8 %all-to-all-done = bf16[4,256,256]{1,2,0:T(8,128)(2,1)S(1)} async-done(((bf16[4,256,256]{1,2,0:T(8,128)(2,1)}), bf16[4,256,256]{1,2,0:T(8,128)(2,1)S(1)}, u32[]{:S(2)}, u32[]{:S(2)}) %all-to-all-start) | async-done | bytes 524320 | tf_op jit(solution)/shard_map/all_to_all | solution.py:172
  294.7 3.5 %all-to-all-start.1 = ((bf16[4,256,256]{1,2,0:T(8,128)(2,1)}), bf16[4,256,256]{1,2,0:T(8,128)(2,1)S(1)}, u32[]{:S(2)}, u32[]{:S(2)}) async-start(bf16[4,256,256]{1,2,0:T(8,128)(2,1)} %copy.21), calls=%async_computation.3 | async-start | bytes 1048576 | tf_op jit(solution)/shard_map/all_to_all | solution.py:173
  298.2 0.2 convert_reduce_fusion
  298.4 8.6 %all-to-all-done.1 = bf16[4,256,256]{1,2,0:T(8,128)(2,1)S(1)} async-done(((bf16[4,256,256]{1,2,0:T(8,128)(2,1)}), bf16[4,256,256]{1,2,0:T(8,128)(2,1)S(1)}, u32[]{:S(2)}, u32[]{:S(2)}) %all-to-all-start.1) | async-done | bytes 524320 | tf_op jit(solution)/shard_map/all_to_all | solution.py:173
  307.0 0.2 fusion
  307.2 1.5 convolution_convert_fusion
  (36 shorter events, 0.8 us)
Async XLA Ops:
  6.5 300.6 %copy-start = (bf16[1024,1024]{1,0:T(8,128)(2,1)S(1)}, bf16[1024,1024]{1,0:T(8,128)(2,1)}, u32[]{:S(2)}) copy-start(bf16[1024,1024]{1,0:T(8,128)(2,1)} %param.9) | copy-start | bytes 6291460
  6.5 27.7 %all-gather.8.cloned.1.call-start = ((), (), s32[]{:S(2)}) async-start(), calls=%async_computation.4 | async-start | bytes 2621440 | tf_op jit(solution)/shard_map/all_gather | solution.py:162
  6.5 35.0 %copy-start.8 = (s32[16]{0:T(128)S(1)}, s32[16]{0:T(128)}, u32[]{:S(2)}) copy-start(s32[16]{0:T(128)} %param.12) | copy-start | bytes 196
  6.5 35.0 %copy-start.9 = (s32[2]{0:T(128)S(1)}, s32[2]{0:T(128)}, u32[]{:S(2)}) copy-start(s32[2]{0:T(128)} %param.11) | copy-start | bytes 28
  6.5 35.3 %copy-start.7 = (s32[64,1]{0,1:T(1,128)S(1)}, s32[64,1]{0,1:T(1,128)}, u32[]{:S(2)}) copy-start(s32[64,1]{0,1:T(1,128)} %param.13) | copy-start | bytes 772
  7.3 83.0 %all-gather.10.cloned.1.call-start = ((), (), s32[]{:S(2)}) async-start(), calls=%async_computation.7 | async-start | bytes 2359296 | tf_op jit(solution)/shard_map/all_gather | solution.py:168
  34.2 1.6 copy-start.5
  35.8 1.2 copy-start.6
  40.7 99.6 %all-gather.12.cloned.1.call-start = ((), (), s32[]{:S(2)}) async-start(), calls=%async_computation.8 | async-start | bytes 2359296 | tf_op jit(solution)/shard_map/all_gather | solution.py:168
  41.5 168.9 %reduce-scatter.3.cloned.1.call-start = ((), (), s32[]{:S(2)}) async-start(), calls=%async_computation.5 | async-start | bytes 2359296 | tf_op jit(solution)/shard_map/reduce_scatter | solution.py:170
  90.2 1.6 copy-start.4
  103.4 1.4 copy-start.1
  104.7 175.6 %reduce-scatter.5.cloned.1.call-start = ((), (), s32[]{:S(2)}) async-start(), calls=%async_computation.6 | async-start | bytes 2359296 | tf_op jit(solution)/shard_map/reduce_scatter | solution.py:170
  140.3 1.6 copy-start.3
  153.4 1.3 copy-start.2
  282.4 12.3 %all-to-all-start = ((bf16[4,256,256]{1,2,0:T(8,128)(2,1)}), bf16[4,256,256]{1,2,0:T(8,128)(2,1)S(1)}, u32[]{:S(2)}, u32[]{:S(2)}) async-start(bf16[4,256,256]{1,2,0:T(8,128)(2,1)} %copy.20), calls=%async_computation.2 | async-start | bytes 1048576 | tf_op jit(solution)/shard_map/all_to_all | solution.py:172
  294.7 12.3 %all-to-all-start.1 = ((bf16[4,256,256]{1,2,0:T(8,128)(2,1)}), bf16[4,256,256]{1,2,0:T(8,128)(2,1)S(1)}, u32[]{:S(2)}, u32[]{:S(2)}) async-start(bf16[4,256,256]{1,2,0:T(8,128)(2,1)} %copy.21), calls=%async_computation.3 | async-start | bytes 1048576 | tf_op jit(solution)/shard_map/all_to_all | solution.py:173
Sparse Core Ops, SparseCore 0:
  8.9 25.2 all-gather.7
  40.8 49.3 all-gather.9
  92.4 47.9 all-gather.11
  143.7 66.5 reduce-scatter.2
  213.7 66.5 reduce-scatter.4
